TPU v7x, 128 devices: a whole 4x4x4 slice. The times are simulated.
128 devices in a mesh: lat: 64 (over z, y, x), lev: 2 (over core).
Axes of the slice: x: 4, y: 4, z: 4, core: 2. Of those that a mesh axis runs over, the one named last changes fastest.
Arguments:
- grid_values: bfloat16 [2560, 64, 5136], P('lat', 'lev'), may hold values from -6 to 6
- lat_counts: int32 [1280], P('lat'), may hold values from 8 to 5136, as said below
- wave_table: int32 [128], replicated, may hold values from 0 to 1279, as said below
- inverses: float32 [2560, 2, 32, 32], P('lat'), may hold values from -1 to 1
- legendre: bfloat16 [128, 2, 640, 1280], P('lat', None, 'lev')
Outputs:
- spectral: bfloat16 [128, 2, 640, 128], P('lat', None, 'lev')
Inputs may be any that keep to these rules, and one draw needn't show every extreme that they name: `lat_counts`: a multiple of 4 on every pair; 8 on the polar pair, 5136 on the pair nearest the equator, 20 + 4 p less 0 to 12 on pair p between. `wave_table`: distinct wavenumbers; 0 and 1279 are always among them.
All inputs are finite; a program needn't handle non-finite values.
Results may differ from a plain program's by a relative error of at most 0.015.
Values may be sent and summed in bfloat16 or wider, within the bound.
No kernel may reach another device: no remote copies, remote signals or barrier semaphores. Data moves between devices by JAX's collectives and lax.ppermute only.
A program may use at most 128 MiB of HBM per device.

v0:
```python
import math
import jax
import jax.numpy as jnp
from jax import lax
from jax.sharding import PartitionSpec as P

TRUNC = 1279


def fourier_table(point_count, wavenumbers, width):
    positions = jnp.arange(width, dtype=jnp.int32)
    phase_index = positions[:, None] * wavenumbers[None, :] % point_count
    angles = phase_index.astype(jnp.float32) * (2.0 * math.pi) / point_count.astype(jnp.float32)
    inside = (positions < point_count)[:, None]
    cosines = jnp.where(inside, jnp.cos(angles), 0.0)
    sines = jnp.where(inside, -jnp.sin(angles), 0.0)
    return jnp.concatenate([cosines, sines], axis=1).astype(jnp.bfloat16)


def mix_levels(fourier, inverses):
    band = fourier.shape[0]
    fields = inverses.shape[1]
    levels = inverses.shape[2]
    slots = fourier.shape[3]
    split_data = fourier.astype(jnp.float32).reshape(band, levels, fields, 2, slots)
    mixed = jnp.einsum("aflk,akfrs->sarlf", inverses, split_data, precision=lax.Precision.HIGHEST)
    return mixed.reshape(slots, band, 2, levels * fields)


def fold_pairs(owned):
    wave_count = owned.shape[0]
    all_lats = owned.shape[1]
    columns = owned.shape[3]
    paired = owned.reshape(wave_count, all_lats // 2, 2, 2 * columns)
    return jnp.stack(
        [paired[:, :, 0] + paired[:, :, 1], paired[:, :, 0] - paired[:, :, 1]], axis=1
    ).astype(jnp.bfloat16)


def on_device(grid_values, lat_counts, wave_table, inverses, legendre):
    pair_total = lat_counts.shape[0]
    slab_width = grid_values.shape[1]
    slot_total = wave_table.shape[0]
    storage = grid_values.shape[2]
    grouped = grid_values.reshape(pair_total, 2 * slab_width, storage)

    def transform(item):
        pair_rows, point_count = item
        basis = fourier_table(point_count, wave_table, storage)
        product = jnp.dot(pair_rows, basis, preferred_element_type=jnp.float32)
        product = product / point_count.astype(jnp.float32)
        return product.astype(jnp.bfloat16).reshape(2, slab_width, 2, slot_total)

    fourier = lax.map(transform, (grouped, lat_counts)).reshape(
        2 * pair_total, slab_width, 2, slot_total
    )
    every_level = lax.all_gather(fourier, "lev", axis=1, tiled=True)
    mixed_band = mix_levels(every_level, inverses)
    own_slab = lax.dynamic_slice_in_dim(
        mixed_band, lax.axis_index("lev") * slab_width, slab_width, 3
    )
    slab_owned = lax.all_to_all(
        own_slab.astype(jnp.bfloat16), "lat", split_axis=0, concat_axis=1, tiled=True
    ).astype(own_slab.dtype)
    owned = lax.all_gather(slab_owned.astype(jnp.bfloat16), "lev", axis=3, tiled=True).astype(
        slab_owned.dtype
    )
    folded = fold_pairs(owned)
    wave_count = folded.shape[0]
    summed = jnp.einsum("wqjp,wqpe->wqje", legendre, folded, preferred_element_type=jnp.float32)
    degree_rows = legendre.shape[2]
    wavenumbers = lax.dynamic_slice_in_dim(
        wave_table, lax.axis_index("lat") * wave_count, wave_count
    )
    steps_index = lax.axis_index("lev") * degree_rows + jnp.arange(degree_rows, dtype=jnp.int32)
    parity = jnp.arange(2, dtype=jnp.int32)
    degree = wavenumbers[:, None, None] + 2 * steps_index[None, None, :] + parity[None, :, None]
    keep = (degree <= TRUNC)[:, :, :, None]
    return jnp.where(keep, summed, 0.0).astype(jnp.bfloat16)


def solution(mesh):
    placed = (
        P("lat", "lev", None),
        P("lat"),
        P(),
        P("lat", None, None, None),
        P("lat", None, "lev", None),
    )
    return jax.shard_map(
        on_device,
        mesh=mesh,
        in_specs=placed,
        out_specs=P("lat", None, "lev", None),
        check_vma=False,
    )
```

profile of v0, /device:TPU:1, one launch (start us, length us, event | category | flops | bytes accessed | tf_op | source)
XLA Modules:
  0.0 989.2 jit_solution(5237779508937216669)
XLA Ops:
  6.5 875.8 %while.10 = (s32[]{:T(128)}, bf16[20,2,32,2,128]{4,1,0,3,2:T(2,128)(2,1)}, bf16[20,64,5136]{2,1,0:T(8,128)(2,1)}, s32[20]{0:T(128)}, s32[128]{0:T(128)}, /*index=5*/s32[]{:T(128)}, s32[]{:T(128)}) while((s32[]{:T(128)}, bf16[20,2,32,2,128]{4,1,0,3,2:T(2,128)(2,1)}, bf16[20,64,5136]{2,1,0:T(8,128)(2,1)}, s32[20]{0:T(128)}, s32[128]{0:T(128)}, ...), condition=%wide.region_1.2_spmd, body=%wide.region_0.1_spmd.sunk | while | flops 184112144 | bytes 6106801 | solution.py:54
  10.5 37.6 %select_convert_fusion.3 = (bf16[5136,128]{1,0:T(8,128)(2,1)S(1)}, bf16[5136,128]{1,0:T(8,128)(2,1)S(1)}) fusion(pred[5136]{0:T(1024)(128)(4,1)S(1)} %iota_compare_fusion.2, f32[]{:T(128)S(6)} %convert_element_type.47, pred[]{:T(512)S(6)} %lt.50, s32[]{:T(128)S(6)} %select_n.53, s32[128]{0:T(128)} %get-tuple-element.102), kind=kLoop, calls=%fused_computation.9.clone.1 | loop fusion | flops 10518528 | bytes 2635289 | tf_op jit(solution)/shard_map/convert
  48.1 1.7 fusion.46
  54.3 37.6 %select_convert_fusion.3 = (bf16[5136,128]{1,0:T(8,128)(2,1)S(1)}, bf16[5136,128]{1,0:T(8,128)(2,1)S(1)}) fusion(pred[5136]{0:T(1024)(128)(4,1)S(1)} %iota_compare_fusion.2, f32[]{:T(128)S(6)} %convert_element_type.47, pred[]{:T(512)S(6)} %lt.50, s32[]{:T(128)S(6)} %select_n.53, s32[128]{0:T(128)} %get-tuple-element.102), kind=kLoop, calls=%fused_computation.9.clone.1 | loop fusion | flops 10518528 | bytes 2635289 | tf_op jit(solution)/shard_map/convert
  98.1 37.6 %select_convert_fusion.3 = (bf16[5136,128]{1,0:T(8,128)(2,1)S(1)}, bf16[5136,128]{1,0:T(8,128)(2,1)S(1)}) fusion(pred[5136]{0:T(1024)(128)(4,1)S(1)} %iota_compare_fusion.2, f32[]{:T(128)S(6)} %convert_element_type.47, pred[]{:T(512)S(6)} %lt.50, s32[]{:T(128)S(6)} %select_n.53, s32[128]{0:T(128)} %get-tuple-element.102), kind=kLoop, calls=%fused_computation.9.clone.1 | loop fusion | flops 10518528 | bytes 2635289 | tf_op jit(solution)/shard_map/convert
  135.7 1.7 fusion.46
  141.9 37.6 %select_convert_fusion.3 = (bf16[5136,128]{1,0:T(8,128)(2,1)S(1)}, bf16[5136,128]{1,0:T(8,128)(2,1)S(1)}) fusion(pred[5136]{0:T(1024)(128)(4,1)S(1)} %iota_compare_fusion.2, f32[]{:T(128)S(6)} %convert_element_type.47, pred[]{:T(512)S(6)} %lt.50, s32[]{:T(128)S(6)} %select_n.53, s32[128]{0:T(128)} %get-tuple-element.102), kind=kLoop, calls=%fused_computation.9.clone.1 | loop fusion | flops 10518528 | bytes 2635289 | tf_op jit(solution)/shard_map/convert
  185.6 37.6 %select_convert_fusion.3 = (bf16[5136,128]{1,0:T(8,128)(2,1)S(1)}, bf16[5136,128]{1,0:T(8,128)(2,1)S(1)}) fusion(pred[5136]{0:T(1024)(128)(4,1)S(1)} %iota_compare_fusion.2, f32[]{:T(128)S(6)} %convert_element_type.47, pred[]{:T(512)S(6)} %lt.50, s32[]{:T(128)S(6)} %select_n.53, s32[128]{0:T(128)} %get-tuple-element.102), kind=kLoop, calls=%fused_computation.9.clone.1 | loop fusion | flops 10518528 | bytes 2635289 | tf_op jit(solution)/shard_map/convert
  223.2 1.7 fusion.46
  229.4 37.6 %select_convert_fusion.3 = (bf16[5136,128]{1,0:T(8,128)(2,1)S(1)}, bf16[5136,128]{1,0:T(8,128)(2,1)S(1)}) fusion(pred[5136]{0:T(1024)(128)(4,1)S(1)} %iota_compare_fusion.2, f32[]{:T(128)S(6)} %convert_element_type.47, pred[]{:T(512)S(6)} %lt.50, s32[]{:T(128)S(6)} %select_n.53, s32[128]{0:T(128)} %get-tuple-element.102), kind=kLoop, calls=%fused_computation.9.clone.1 | loop fusion | flops 10518528 | bytes 2635289 | tf_op jit(solution)/shard_map/convert
  267.0 1.7 fusion.46
  273.2 37.6 %select_convert_fusion.3 = (bf16[5136,128]{1,0:T(8,128)(2,1)S(1)}, bf16[5136,128]{1,0:T(8,128)(2,1)S(1)}) fusion(pred[5136]{0:T(1024)(128)(4,1)S(1)} %iota_compare_fusion.2, f32[]{:T(128)S(6)} %convert_element_type.47, pred[]{:T(512)S(6)} %lt.50, s32[]{:T(128)S(6)} %select_n.53, s32[128]{0:T(128)} %get-tuple-element.102), kind=kLoop, calls=%fused_computation.9.clone.1 | loop fusion | flops 10518528 | bytes 2635289 | tf_op jit(solution)/shard_map/convert
  310.8 1.7 fusion.46
  317.0 37.6 %select_convert_fusion.3 = (bf16[5136,128]{1,0:T(8,128)(2,1)S(1)}, bf16[5136,128]{1,0:T(8,128)(2,1)S(1)}) fusion(pred[5136]{0:T(1024)(128)(4,1)S(1)} %iota_compare_fusion.2, f32[]{:T(128)S(6)} %convert_element_type.47, pred[]{:T(512)S(6)} %lt.50, s32[]{:T(128)S(6)} %select_n.53, s32[128]{0:T(128)} %get-tuple-element.102), kind=kLoop, calls=%fused_computation.9.clone.1 | loop fusion | flops 10518528 | bytes 2635289 | tf_op jit(solution)/shard_map/convert
  354.5 1.7 fusion.46
  360.7 37.6 %select_convert_fusion.3 = (bf16[5136,128]{1,0:T(8,128)(2,1)S(1)}, bf16[5136,128]{1,0:T(8,128)(2,1)S(1)}) fusion(pred[5136]{0:T(1024)(128)(4,1)S(1)} %iota_compare_fusion.2, f32[]{:T(128)S(6)} %convert_element_type.47, pred[]{:T(512)S(6)} %lt.50, s32[]{:T(128)S(6)} %select_n.53, s32[128]{0:T(128)} %get-tuple-element.102), kind=kLoop, calls=%fused_computation.9.clone.1 | loop fusion | flops 10518528 | bytes 2635289 | tf_op jit(solution)/shard_map/convert
  404.5 37.6 %select_convert_fusion.3 = (bf16[5136,128]{1,0:T(8,128)(2,1)S(1)}, bf16[5136,128]{1,0:T(8,128)(2,1)S(1)}) fusion(pred[5136]{0:T(1024)(128)(4,1)S(1)} %iota_compare_fusion.2, f32[]{:T(128)S(6)} %convert_element_type.47, pred[]{:T(512)S(6)} %lt.50, s32[]{:T(128)S(6)} %select_n.53, s32[128]{0:T(128)} %get-tuple-element.102), kind=kLoop, calls=%fused_computation.9.clone.1 | loop fusion | flops 10518528 | bytes 2635289 | tf_op jit(solution)/shard_map/convert
  442.1 1.7 fusion.46
  448.3 37.6 %select_convert_fusion.3 = (bf16[5136,128]{1,0:T(8,128)(2,1)S(1)}, bf16[5136,128]{1,0:T(8,128)(2,1)S(1)}) fusion(pred[5136]{0:T(1024)(128)(4,1)S(1)} %iota_compare_fusion.2, f32[]{:T(128)S(6)} %convert_element_type.47, pred[]{:T(512)S(6)} %lt.50, s32[]{:T(128)S(6)} %select_n.53, s32[128]{0:T(128)} %get-tuple-element.102), kind=kLoop, calls=%fused_computation.9.clone.1 | loop fusion | flops 10518528 | bytes 2635289 | tf_op jit(solution)/shard_map/convert
  485.9 1.7 fusion.46
  492.1 37.6 %select_convert_fusion.3 = (bf16[5136,128]{1,0:T(8,128)(2,1)S(1)}, bf16[5136,128]{1,0:T(8,128)(2,1)S(1)}) fusion(pred[5136]{0:T(1024)(128)(4,1)S(1)} %iota_compare_fusion.2, f32[]{:T(128)S(6)} %convert_element_type.47, pred[]{:T(512)S(6)} %lt.50, s32[]{:T(128)S(6)} %select_n.53, s32[128]{0:T(128)} %get-tuple-element.102), kind=kLoop, calls=%fused_computation.9.clone.1 | loop fusion | flops 10518528 | bytes 2635289 | tf_op jit(solution)/shard_map/convert
  529.7 1.7 fusion.46
  535.9 37.6 %select_convert_fusion.3 = (bf16[5136,128]{1,0:T(8,128)(2,1)S(1)}, bf16[5136,128]{1,0:T(8,128)(2,1)S(1)}) fusion(pred[5136]{0:T(1024)(128)(4,1)S(1)} %iota_compare_fusion.2, f32[]{:T(128)S(6)} %convert_element_type.47, pred[]{:T(512)S(6)} %lt.50, s32[]{:T(128)S(6)} %select_n.53, s32[128]{0:T(128)} %get-tuple-element.102), kind=kLoop, calls=%fused_computation.9.clone.1 | loop fusion | flops 10518528 | bytes 2635289 | tf_op jit(solution)/shard_map/convert
  573.5 1.7 fusion.46
  579.7 37.6 %select_convert_fusion.3 = (bf16[5136,128]{1,0:T(8,128)(2,1)S(1)}, bf16[5136,128]{1,0:T(8,128)(2,1)S(1)}) fusion(pred[5136]{0:T(1024)(128)(4,1)S(1)} %iota_compare_fusion.2, f32[]{:T(128)S(6)} %convert_element_type.47, pred[]{:T(512)S(6)} %lt.50, s32[]{:T(128)S(6)} %select_n.53, s32[128]{0:T(128)} %get-tuple-element.102), kind=kLoop, calls=%fused_computation.9.clone.1 | loop fusion | flops 10518528 | bytes 2635289 | tf_op jit(solution)/shard_map/convert
  617.3 1.7 fusion.46
  623.5 37.6 %select_convert_fusion.3 = (bf16[5136,128]{1,0:T(8,128)(2,1)S(1)}, bf16[5136,128]{1,0:T(8,128)(2,1)S(1)}) fusion(pred[5136]{0:T(1024)(128)(4,1)S(1)} %iota_compare_fusion.2, f32[]{:T(128)S(6)} %convert_element_type.47, pred[]{:T(512)S(6)} %lt.50, s32[]{:T(128)S(6)} %select_n.53, s32[128]{0:T(128)} %get-tuple-element.102), kind=kLoop, calls=%fused_computation.9.clone.1 | loop fusion | flops 10518528 | bytes 2635289 | tf_op jit(solution)/shard_map/convert
  661.1 1.7 fusion.46
  667.3 37.6 %select_convert_fusion.3 = (bf16[5136,128]{1,0:T(8,128)(2,1)S(1)}, bf16[5136,128]{1,0:T(8,128)(2,1)S(1)}) fusion(pred[5136]{0:T(1024)(128)(4,1)S(1)} %iota_compare_fusion.2, f32[]{:T(128)S(6)} %convert_element_type.47, pred[]{:T(512)S(6)} %lt.50, s32[]{:T(128)S(6)} %select_n.53, s32[128]{0:T(128)} %get-tuple-element.102), kind=kLoop, calls=%fused_computation.9.clone.1 | loop fusion | flops 10518528 | bytes 2635289 | tf_op jit(solution)/shard_map/convert
  704.9 1.7 fusion.46
  711.1 37.6 %select_convert_fusion.3 = (bf16[5136,128]{1,0:T(8,128)(2,1)S(1)}, bf16[5136,128]{1,0:T(8,128)(2,1)S(1)}) fusion(pred[5136]{0:T(1024)(128)(4,1)S(1)} %iota_compare_fusion.2, f32[]{:T(128)S(6)} %convert_element_type.47, pred[]{:T(512)S(6)} %lt.50, s32[]{:T(128)S(6)} %select_n.53, s32[128]{0:T(128)} %get-tuple-element.102), kind=kLoop, calls=%fused_computation.9.clone.1 | loop fusion | flops 10518528 | bytes 2635289 | tf_op jit(solution)/shard_map/convert
  754.8 37.6 %select_convert_fusion.3 = (bf16[5136,128]{1,0:T(8,128)(2,1)S(1)}, bf16[5136,128]{1,0:T(8,128)(2,1)S(1)}) fusion(pred[5136]{0:T(1024)(128)(4,1)S(1)} %iota_compare_fusion.2, f32[]{:T(128)S(6)} %convert_element_type.47, pred[]{:T(512)S(6)} %lt.50, s32[]{:T(128)S(6)} %select_n.53, s32[128]{0:T(128)} %get-tuple-element.102), kind=kLoop, calls=%fused_computation.9.clone.1 | loop fusion | flops 10518528 | bytes 2635289 | tf_op jit(solution)/shard_map/convert
  798.6 37.6 %select_convert_fusion.3 = (bf16[5136,128]{1,0:T(8,128)(2,1)S(1)}, bf16[5136,128]{1,0:T(8,128)(2,1)S(1)}) fusion(pred[5136]{0:T(1024)(128)(4,1)S(1)} %iota_compare_fusion.2, f32[]{:T(128)S(6)} %convert_element_type.47, pred[]{:T(512)S(6)} %lt.50, s32[]{:T(128)S(6)} %select_n.53, s32[128]{0:T(128)} %get-tuple-element.102), kind=kLoop, calls=%fused_computation.9.clone.1 | loop fusion | flops 10518528 | bytes 2635289 | tf_op jit(solution)/shard_map/convert
  842.4 37.6 %select_convert_fusion.3 = (bf16[5136,128]{1,0:T(8,128)(2,1)S(1)}, bf16[5136,128]{1,0:T(8,128)(2,1)S(1)}) fusion(pred[5136]{0:T(1024)(128)(4,1)S(1)} %iota_compare_fusion.2, f32[]{:T(128)S(6)} %convert_element_type.47, pred[]{:T(512)S(6)} %lt.50, s32[]{:T(128)S(6)} %select_n.53, s32[128]{0:T(128)} %get-tuple-element.102), kind=kLoop, calls=%fused_computation.9.clone.1 | loop fusion | flops 10518528 | bytes 2635289 | tf_op jit(solution)/shard_map/convert
  882.6 3.2 copy.37
  885.9 12.4 %all-gather.3.cloned.1.call-done = bf16[40,64,2,128]{3,0,2,1:T(8,128)(2,1)} async-done(((bf16[40,32,2,128]{3,0,2,1:T(8,128)(2,1)}), bf16[40,64,2,128]{3,0,2,1:T(8,128)(2,1)}) %all-gather.3.cloned.1.call-update) | async-done | bytes 1310736 | tf_op jit(solution)/shard_map/all_gather | solution.py:57
  898.3 3.2 convolution_bitcast_fusion
  903.3 4.7 copy.31
  908.0 5.7 reshape.111
  913.7 24.2 %all_to_all.18 = bf16[64,2,2560]{2,1,0:T(2,128)(2,1)} all-to-all(bf16[64,2,2560]{2,1,0:T(2,128)(2,1)} %reshape.111), channel_id=1, replica_groups=mesh['lat'=64,'lev'=2] {'lat'}, dimensions={0} | all-to-all | bytes 1310720 | tf_op jit(solution)/shard_map/all_to_all | solution.py:62
  937.9 5.8 reshape.112
  943.7 4.3 copy.32
  948.0 4.7 all_to_all.16
  952.9 9.2 all-gather.5.cloned.1.call-done
  962.0 6.6 copy.33
  968.6 7.3 reshape.109
  975.9 4.4 fusion.38
  980.6 1.8 fusion.32
  (103 shorter events, 66.6 us)
Async XLA Ops:
  6.5 974.0 %copy-start = (bf16[2,2,320,1280]{3,2,1,0:T(8,128)(2,1)S(1)}, bf16[2,2,320,1280]{3,2,1,0:T(8,128)(2,1)}, u32[]{:S(2)}) copy-start(bf16[2,2,320,1280]{3,2,1,0:T(8,128)(2,1)} %param.11) | copy-start | bytes 9830404
  6.5 891.8 %all-gather.3.cloned.1.call-start = ((), (), s32[]{:S(2)}) async-start(), calls=%async_computation.1 | async-start | bytes 1966080 | tf_op jit(solution)/shard_map/all_gather | solution.py:57
  882.4 79.6 %all-gather.5.cloned.1.call-start = ((), (), s32[]{:S(2)}) async-start(), calls=%async_computation.2 | async-start | bytes 1966080 | tf_op jit(solution)/shard_map/all_gather | solution.py:65
  948.0 4.7 copy-start.1
Sparse Core Ops, SparseCore 0:
  882.5 15.7 all-gather.2
  952.8 9.1 all-gather.4
where the time goes:
time: 992 us; the launch traced here: 989 us
  other arithmetic  764 us (77%)
  local copies, waits for them, and re-layouts  88.3 us (9%)
  matrix products  38.9 us (4%)
  loops' own time  38 us (4%)
  blocking collectives  24.2 us (2%)
  waiting for transfers between devices  21.7 us (2%)
  between operations  13.5 us (1%)
    another operation x20, other arithmetic  751 us
    another operation x1, loops' own time, on_device(): lax.map(transform, (grouped, lat_counts))  38 us
    dot_general x20, matrix products, transform(): product = jnp.dot(pair_rows, basis, preferred_element_type=jnp.float32)  34 us
    dynamic_slice x20, local copies, waits for them, and re-layouts, on_device(): lax.map(transform, (grouped, lat_counts))  26.2 us
    all_to_all x1, blocking collectives, on_device(): lax.all_to_all(own_slab.astype(jnp.bfloat16), 'lat', split_axis=0, concat...  24.2 us
  transfers between devices with their start and end apart: 2, of which 2 were waited for; matrix products, arithmetic and copies ran while one was open for 0% of the time, Pallas kernels for 0%

commit v1 on v0

--- a/solution.py
+++ b/solution.py
@@ -1,10 +1,22 @@
+import functools
 import math
 import jax
 import jax.numpy as jnp
 from jax import lax
 from jax.sharding import PartitionSpec as P
+from jax.lax import all_to_all, psum
 
 TRUNC = 1279
+
+
+def ticks_open(message, peer_axis, dim_at, on_dim):
+    return jnp.concatenate(
+        all_to_all(jnp.stack(jnp.split(message, psum(1, peer_axis), dim_at), 0), peer_axis, 0, 0),
+        on_dim,
+    )
+
+
+_view_series_all = functools.partial(ticks_open, peer_axis="lat", dim_at=0, on_dim=1)
 
 
 def fourier_table(point_count, wavenumbers, width):
@@ -59,9 +71,7 @@
     own_slab = lax.dynamic_slice_in_dim(
         mixed_band, lax.axis_index("lev") * slab_width, slab_width, 3
     )
-    slab_owned = lax.all_to_all(
-        own_slab.astype(jnp.bfloat16), "lat", split_axis=0, concat_axis=1, tiled=True
-    ).astype(own_slab.dtype)
+    slab_owned = _view_series_all(own_slab.astype(jnp.bfloat16)).astype(own_slab.dtype)
     owned = lax.all_gather(slab_owned.astype(jnp.bfloat16), "lev", axis=3, tiled=True).astype(
         slab_owned.dtype
     )

time: 992 us -> 1100 us (1.11)
  local copies, waits for them, and re-layouts: 88.3 us -> 191 us
    unnamed x7 -> x70, local copies, waits for them, and re-layouts: 14.8 us -> 83.6 us
    another operation x0 -> x2, local copies, waits for them, and re-layouts: none -> 39.3 us  [ticks_open(): jnp.stack(jnp.split(message, psum(1, peer_axis), dim_at), 0)]
where the time goes in v1:
time: 1100 us; the launch traced here: 1090 us
  other arithmetic  764 us (69%)
  local copies, waits for them, and re-layouts  191 us (17%)
  matrix products  38.9 us (4%)
  loops' own time  38 us (3%)
  blocking collectives  24.4 us (2%)
  waiting for transfers between devices  21.4 us (2%)
  between operations  13.7 us (1%)
    another operation x20, other arithmetic  751 us
    unnamed x70, local copies, waits for them, and re-layouts  83.6 us
    another operation x2, local copies, waits for them, and re-layouts, ticks_open(): jnp.stack(jnp.split(message, psum(1, peer_axis), dim_at), 0)  39.3 us
    another operation x1, loops' own time, on_device(): lax.map(transform, (grouped, lat_counts))  38 us
    dot_general x20, matrix products, transform(): product = jnp.dot(pair_rows, basis, preferred_element_type=jnp.float32)  34 us
    dynamic_slice x20, local copies, waits for them, and re-layouts, on_device(): lax.map(transform, (grouped, lat_counts))  26.2 us
    all_to_all x1, blocking collectives, ticks_open(): all_to_all(jnp.stack(jnp.split(message, psum(1, peer_axis), dim_at), 0),...  24.4 us
  transfers between devices with their start and end apart: 2, of which 2 were waited for; matrix products, arithmetic and copies ran while one was open for 0% of the time, Pallas kernels for 0%

profile of v1, /device:TPU:1, one launch (start us, length us, event | category | flops | bytes accessed | tf_op | source)
XLA Modules:
  0.0 1092.7 jit_solution(3769817812661145225)
XLA Ops:
  6.5 875.8 %while.10 = (s32[]{:T(128)}, bf16[20,2,32,2,128]{4,1,0,3,2:T(2,128)(2,1)}, bf16[20,64,5136]{2,1,0:T(8,128)(2,1)}, s32[20]{0:T(128)}, s32[128]{0:T(128)}, /*index=5*/s32[]{:T(128)}, s32[]{:T(128)}) while((s32[]{:T(128)}, bf16[20,2,32,2,128]{4,1,0,3,2:T(2,128)(2,1)}, bf16[20,64,5136]{2,1,0:T(8,128)(2,1)}, s32[20]{0:T(128)}, s32[128]{0:T(128)}, ...), condition=%wide.region_1.2_spmd, body=%wide.region_0.1_spmd.sunk | while | flops 184112144 | bytes 6106801 | solution.py:66
  10.5 37.6 %select_convert_fusion.3 = (bf16[5136,128]{1,0:T(8,128)(2,1)S(1)}, bf16[5136,128]{1,0:T(8,128)(2,1)S(1)}) fusion(pred[5136]{0:T(1024)(128)(4,1)S(1)} %iota_compare_fusion.2, f32[]{:T(128)S(6)} %convert_element_type.47, pred[]{:T(512)S(6)} %lt.50, s32[]{:T(128)S(6)} %select_n.53, s32[128]{0:T(128)} %get-tuple-element.102), kind=kLoop, calls=%fused_computation.9.clone.1 | loop fusion | flops 10518528 | bytes 2635289 | tf_op jit(solution)/shard_map/convert
  48.1 1.7 fusion.110
  54.3 37.6 %select_convert_fusion.3 = (bf16[5136,128]{1,0:T(8,128)(2,1)S(1)}, bf16[5136,128]{1,0:T(8,128)(2,1)S(1)}) fusion(pred[5136]{0:T(1024)(128)(4,1)S(1)} %iota_compare_fusion.2, f32[]{:T(128)S(6)} %convert_element_type.47, pred[]{:T(512)S(6)} %lt.50, s32[]{:T(128)S(6)} %select_n.53, s32[128]{0:T(128)} %get-tuple-element.102), kind=kLoop, calls=%fused_computation.9.clone.1 | loop fusion | flops 10518528 | bytes 2635289 | tf_op jit(solution)/shard_map/convert
  98.1 37.6 %select_convert_fusion.3 = (bf16[5136,128]{1,0:T(8,128)(2,1)S(1)}, bf16[5136,128]{1,0:T(8,128)(2,1)S(1)}) fusion(pred[5136]{0:T(1024)(128)(4,1)S(1)} %iota_compare_fusion.2, f32[]{:T(128)S(6)} %convert_element_type.47, pred[]{:T(512)S(6)} %lt.50, s32[]{:T(128)S(6)} %select_n.53, s32[128]{0:T(128)} %get-tuple-element.102), kind=kLoop, calls=%fused_computation.9.clone.1 | loop fusion | flops 10518528 | bytes 2635289 | tf_op jit(solution)/shard_map/convert
  135.7 1.7 fusion.110
  141.9 37.6 %select_convert_fusion.3 = (bf16[5136,128]{1,0:T(8,128)(2,1)S(1)}, bf16[5136,128]{1,0:T(8,128)(2,1)S(1)}) fusion(pred[5136]{0:T(1024)(128)(4,1)S(1)} %iota_compare_fusion.2, f32[]{:T(128)S(6)} %convert_element_type.47, pred[]{:T(512)S(6)} %lt.50, s32[]{:T(128)S(6)} %select_n.53, s32[128]{0:T(128)} %get-tuple-element.102), kind=kLoop, calls=%fused_computation.9.clone.1 | loop fusion | flops 10518528 | bytes 2635289 | tf_op jit(solution)/shard_map/convert
  185.6 37.6 %select_convert_fusion.3 = (bf16[5136,128]{1,0:T(8,128)(2,1)S(1)}, bf16[5136,128]{1,0:T(8,128)(2,1)S(1)}) fusion(pred[5136]{0:T(1024)(128)(4,1)S(1)} %iota_compare_fusion.2, f32[]{:T(128)S(6)} %convert_element_type.47, pred[]{:T(512)S(6)} %lt.50, s32[]{:T(128)S(6)} %select_n.53, s32[128]{0:T(128)} %get-tuple-element.102), kind=kLoop, calls=%fused_computation.9.clone.1 | loop fusion | flops 10518528 | bytes 2635289 | tf_op jit(solution)/shard_map/convert
  223.2 1.7 fusion.110
  229.4 37.6 %select_convert_fusion.3 = (bf16[5136,128]{1,0:T(8,128)(2,1)S(1)}, bf16[5136,128]{1,0:T(8,128)(2,1)S(1)}) fusion(pred[5136]{0:T(1024)(128)(4,1)S(1)} %iota_compare_fusion.2, f32[]{:T(128)S(6)} %convert_element_type.47, pred[]{:T(512)S(6)} %lt.50, s32[]{:T(128)S(6)} %select_n.53, s32[128]{0:T(128)} %get-tuple-element.102), kind=kLoop, calls=%fused_computation.9.clone.1 | loop fusion | flops 10518528 | bytes 2635289 | tf_op jit(solution)/shard_map/convert
  267.0 1.7 fusion.110
  273.2 37.6 %select_convert_fusion.3 = (bf16[5136,128]{1,0:T(8,128)(2,1)S(1)}, bf16[5136,128]{1,0:T(8,128)(2,1)S(1)}) fusion(pred[5136]{0:T(1024)(128)(4,1)S(1)} %iota_compare_fusion.2, f32[]{:T(128)S(6)} %convert_element_type.47, pred[]{:T(512)S(6)} %lt.50, s32[]{:T(128)S(6)} %select_n.53, s32[128]{0:T(128)} %get-tuple-element.102), kind=kLoop, calls=%fused_computation.9.clone.1 | loop fusion | flops 10518528 | bytes 2635289 | tf_op jit(solution)/shard_map/convert
  310.8 1.7 fusion.110
  317.0 37.6 %select_convert_fusion.3 = (bf16[5136,128]{1,0:T(8,128)(2,1)S(1)}, bf16[5136,128]{1,0:T(8,128)(2,1)S(1)}) fusion(pred[5136]{0:T(1024)(128)(4,1)S(1)} %iota_compare_fusion.2, f32[]{:T(128)S(6)} %convert_element_type.47, pred[]{:T(512)S(6)} %lt.50, s32[]{:T(128)S(6)} %select_n.53, s32[128]{0:T(128)} %get-tuple-element.102), kind=kLoop, calls=%fused_computation.9.clone.1 | loop fusion | flops 10518528 | bytes 2635289 | tf_op jit(solution)/shard_map/convert
  354.5 1.7 fusion.110
  360.7 37.6 %select_convert_fusion.3 = (bf16[5136,128]{1,0:T(8,128)(2,1)S(1)}, bf16[5136,128]{1,0:T(8,128)(2,1)S(1)}) fusion(pred[5136]{0:T(1024)(128)(4,1)S(1)} %iota_compare_fusion.2, f32[]{:T(128)S(6)} %convert_element_type.47, pred[]{:T(512)S(6)} %lt.50, s32[]{:T(128)S(6)} %select_n.53, s32[128]{0:T(128)} %get-tuple-element.102), kind=kLoop, calls=%fused_computation.9.clone.1 | loop fusion | flops 10518528 | bytes 2635289 | tf_op jit(solution)/shard_map/convert
  404.5 37.6 %select_convert_fusion.3 = (bf16[5136,128]{1,0:T(8,128)(2,1)S(1)}, bf16[5136,128]{1,0:T(8,128)(2,1)S(1)}) fusion(pred[5136]{0:T(1024)(128)(4,1)S(1)} %iota_compare_fusion.2, f32[]{:T(128)S(6)} %convert_element_type.47, pred[]{:T(512)S(6)} %lt.50, s32[]{:T(128)S(6)} %select_n.53, s32[128]{0:T(128)} %get-tuple-element.102), kind=kLoop, calls=%fused_computation.9.clone.1 | loop fusion | flops 10518528 | bytes 2635289 | tf_op jit(solution)/shard_map/convert
  442.1 1.7 fusion.110
  448.3 37.6 %select_convert_fusion.3 = (bf16[5136,128]{1,0:T(8,128)(2,1)S(1)}, bf16[5136,128]{1,0:T(8,128)(2,1)S(1)}) fusion(pred[5136]{0:T(1024)(128)(4,1)S(1)} %iota_compare_fusion.2, f32[]{:T(128)S(6)} %convert_element_type.47, pred[]{:T(512)S(6)} %lt.50, s32[]{:T(128)S(6)} %select_n.53, s32[128]{0:T(128)} %get-tuple-element.102), kind=kLoop, calls=%fused_computation.9.clone.1 | loop fusion | flops 10518528 | bytes 2635289 | tf_op jit(solution)/shard_map/convert
  485.9 1.7 fusion.110
  492.1 37.6 %select_convert_fusion.3 = (bf16[5136,128]{1,0:T(8,128)(2,1)S(1)}, bf16[5136,128]{1,0:T(8,128)(2,1)S(1)}) fusion(pred[5136]{0:T(1024)(128)(4,1)S(1)} %iota_compare_fusion.2, f32[]{:T(128)S(6)} %convert_element_type.47, pred[]{:T(512)S(6)} %lt.50, s32[]{:T(128)S(6)} %select_n.53, s32[128]{0:T(128)} %get-tuple-element.102), kind=kLoop, calls=%fused_computation.9.clone.1 | loop fusion | flops 10518528 | bytes 2635289 | tf_op jit(solution)/shard_map/convert
  529.7 1.7 fusion.110
  535.9 37.6 %select_convert_fusion.3 = (bf16[5136,128]{1,0:T(8,128)(2,1)S(1)}, bf16[5136,128]{1,0:T(8,128)(2,1)S(1)}) fusion(pred[5136]{0:T(1024)(128)(4,1)S(1)} %iota_compare_fusion.2, f32[]{:T(128)S(6)} %convert_element_type.47, pred[]{:T(512)S(6)} %lt.50, s32[]{:T(128)S(6)} %select_n.53, s32[128]{0:T(128)} %get-tuple-element.102), kind=kLoop, calls=%fused_computation.9.clone.1 | loop fusion | flops 10518528 | bytes 2635289 | tf_op jit(solution)/shard_map/convert
  573.5 1.7 fusion.110
  579.7 37.6 %select_convert_fusion.3 = (bf16[5136,128]{1,0:T(8,128)(2,1)S(1)}, bf16[5136,128]{1,0:T(8,128)(2,1)S(1)}) fusion(pred[5136]{0:T(1024)(128)(4,1)S(1)} %iota_compare_fusion.2, f32[]{:T(128)S(6)} %convert_element_type.47, pred[]{:T(512)S(6)} %lt.50, s32[]{:T(128)S(6)} %select_n.53, s32[128]{0:T(128)} %get-tuple-element.102), kind=kLoop, calls=%fused_computation.9.clone.1 | loop fusion | flops 10518528 | bytes 2635289 | tf_op jit(solution)/shard_map/convert
  617.3 1.7 fusion.110
  623.5 37.6 %select_convert_fusion.3 = (bf16[5136,128]{1,0:T(8,128)(2,1)S(1)}, bf16[5136,128]{1,0:T(8,128)(2,1)S(1)}) fusion(pred[5136]{0:T(1024)(128)(4,1)S(1)} %iota_compare_fusion.2, f32[]{:T(128)S(6)} %convert_element_type.47, pred[]{:T(512)S(6)} %lt.50, s32[]{:T(128)S(6)} %select_n.53, s32[128]{0:T(128)} %get-tuple-element.102), kind=kLoop, calls=%fused_computation.9.clone.1 | loop fusion | flops 10518528 | bytes 2635289 | tf_op jit(solution)/shard_map/convert
  667.3 37.6 %select_convert_fusion.3 = (bf16[5136,128]{1,0:T(8,128)(2,1)S(1)}, bf16[5136,128]{1,0:T(8,128)(2,1)S(1)}) fusion(pred[5136]{0:T(1024)(128)(4,1)S(1)} %iota_compare_fusion.2, f32[]{:T(128)S(6)} %convert_element_type.47, pred[]{:T(512)S(6)} %lt.50, s32[]{:T(128)S(6)} %select_n.53, s32[128]{0:T(128)} %get-tuple-element.102), kind=kLoop, calls=%fused_computation.9.clone.1 | loop fusion | flops 10518528 | bytes 2635289 | tf_op jit(solution)/shard_map/convert
  704.9 1.7 fusion.110
  711.1 37.6 %select_convert_fusion.3 = (bf16[5136,128]{1,0:T(8,128)(2,1)S(1)}, bf16[5136,128]{1,0:T(8,128)(2,1)S(1)}) fusion(pred[5136]{0:T(1024)(128)(4,1)S(1)} %iota_compare_fusion.2, f32[]{:T(128)S(6)} %convert_element_type.47, pred[]{:T(512)S(6)} %lt.50, s32[]{:T(128)S(6)} %select_n.53, s32[128]{0:T(128)} %get-tuple-element.102), kind=kLoop, calls=%fused_computation.9.clone.1 | loop fusion | flops 10518528 | bytes 2635289 | tf_op jit(solution)/shard_map/convert
  754.8 37.6 %select_convert_fusion.3 = (bf16[5136,128]{1,0:T(8,128)(2,1)S(1)}, bf16[5136,128]{1,0:T(8,128)(2,1)S(1)}) fusion(pred[5136]{0:T(1024)(128)(4,1)S(1)} %iota_compare_fusion.2, f32[]{:T(128)S(6)} %convert_element_type.47, pred[]{:T(512)S(6)} %lt.50, s32[]{:T(128)S(6)} %select_n.53, s32[128]{0:T(128)} %get-tuple-element.102), kind=kLoop, calls=%fused_computation.9.clone.1 | loop fusion | flops 10518528 | bytes 2635289 | tf_op jit(solution)/shard_map/convert
  798.6 37.6 %select_convert_fusion.3 = (bf16[5136,128]{1,0:T(8,128)(2,1)S(1)}, bf16[5136,128]{1,0:T(8,128)(2,1)S(1)}) fusion(pred[5136]{0:T(1024)(128)(4,1)S(1)} %iota_compare_fusion.2, f32[]{:T(128)S(6)} %convert_element_type.47, pred[]{:T(512)S(6)} %lt.50, s32[]{:T(128)S(6)} %select_n.53, s32[128]{0:T(128)} %get-tuple-element.102), kind=kLoop, calls=%fused_computation.9.clone.1 | loop fusion | flops 10518528 | bytes 2635289 | tf_op jit(solution)/shard_map/convert
  842.4 37.6 %select_convert_fusion.3 = (bf16[5136,128]{1,0:T(8,128)(2,1)S(1)}, bf16[5136,128]{1,0:T(8,128)(2,1)S(1)}) fusion(pred[5136]{0:T(1024)(128)(4,1)S(1)} %iota_compare_fusion.2, f32[]{:T(128)S(6)} %convert_element_type.47, pred[]{:T(512)S(6)} %lt.50, s32[]{:T(128)S(6)} %select_n.53, s32[128]{0:T(128)} %get-tuple-element.102), kind=kLoop, calls=%fused_computation.9.clone.1 | loop fusion | flops 10518528 | bytes 2635289 | tf_op jit(solution)/shard_map/convert
  882.9 3.2 copy.101
  886.2 12.2 %all-gather.3.cloned.1.call-done = bf16[40,64,2,128]{3,0,2,1:T(8,128)(2,1)} async-done(((bf16[40,32,2,128]{3,0,2,1:T(8,128)(2,1)}), bf16[40,64,2,128]{3,0,2,1:T(8,128)(2,1)}) %all-gather.3.cloned.1.call-update) | async-done | bytes 1310736 | tf_op jit(solution)/shard_map/all_gather | solution.py:69
  898.3 3.2 convolution_bitcast_fusion
  972.4 38.2 %copy.95 = bf16[64,2,40,2,32]{2,4,3,1,0:T(8,128)(2,1)} copy(bf16[64,2,40,2,32]{1,2,4,3,0:T(8,128)(2,1)} %fusion.37) | data formatting | bytes 1310720 | tf_op jit(solution)/shard_map/stack | solution.py:14
  1010.6 5.7 reshape.119
  1016.3 24.4 %all_to_all.5 = bf16[64,2,2560]{2,1,0:T(2,128)(2,1)} all-to-all(bf16[64,2,2560]{2,1,0:T(2,128)(2,1)} %reshape.119), channel_id=1, replica_groups=mesh['lat'=64,'lev'=2] {'lat'}, dimensions={0} | all-to-all | bytes 1310720 | tf_op jit(solution)/shard_map/all_to_all | solution.py:14
  1040.8 5.8 reshape.120
  1046.6 2.1 bitcast_bitcast_fusion
  1048.7 2.7 copy.96
  1051.3 4.6 reshape.113
  1056.2 9.2 all-gather.5.cloned.1.call-done
  1065.3 6.6 copy.97
  1071.9 7.3 reshape.117
  1079.2 4.4 fusion.102
  1083.9 1.8 fusion.32
  (168 shorter events, 137.7 us)
Async XLA Ops:
  6.5 1077.3 %copy-start = (bf16[2,2,320,1280]{3,2,1,0:T(8,128)(2,1)S(1)}, bf16[2,2,320,1280]{3,2,1,0:T(8,128)(2,1)}, u32[]{:S(2)}) copy-start(bf16[2,2,320,1280]{3,2,1,0:T(8,128)(2,1)} %param.11) | copy-start | bytes 9830404
  6.5 891.8 %all-gather.3.cloned.1.call-start = ((), (), s32[]{:S(2)}) async-start(), calls=%async_computation.1 | async-start | bytes 1966080 | tf_op jit(solution)/shard_map/all_gather | solution.py:69
  882.4 182.9 %all-gather.5.cloned.1.call-start = ((), (), s32[]{:S(2)}) async-start(), calls=%async_computation.2 | async-start | bytes 1966080 | tf_op jit(solution)/shard_map/all_gather | solution.py:75
  954.9 101.1 %copy-start.1 = (s32[128]{0:T(128)S(1)}, s32[128]{0:T(128)}, u32[]{:S(2)}) copy-start(s32[128]{0:T(128)} %get-tuple-element.113) | copy-start | bytes 1540
Sparse Core Ops, SparseCore 0:
  882.5 15.7 all-gather.2
  1056.1 9.1 all-gather.4
